TPU v7x, 256 devices: a whole 4x4x8 slice. The times are simulated.
256 devices in a mesh: resp: 16 (over y, z_hi), ctx: 16 (over x, z_lo, core).
Axes of the slice: x: 4, y: 4, z: 8 (z_hi: 4, z_lo: 2; z = z_hi * 2 + z_lo), core: 2. Of those that a mesh axis runs over, the one named last changes fastest.
Arguments:
- queries: bfloat16 [16, 2048, 2560], P('resp', 'ctx'), may hold values from -96 to 96
- resp_keys: bfloat16 [16, 2048, 512], P('resp', 'ctx'), may hold values from -6 to 6
- resp_values: bfloat16 [16, 2048, 512], P('resp', 'ctx'), may hold values from -6 to 6
- prompt_keys: bfloat16 [512, 512], P('ctx'), may hold values from -6 to 6
- prompt_values: bfloat16 [512, 512], P('ctx'), may hold values from -6 to 6
- out_grad: bfloat16 [16, 2048, 2560], P('resp', 'ctx'), may hold values from -24 to 24
- lengths: int32 [16], P('resp'), may hold values from 256 to 2048, as said below
Outputs:
- attn_out: bfloat16 [16, 2048, 2560], P('resp', 'ctx')
- query_grad: bfloat16 [16, 2048, 2560], P('resp', 'ctx')
- resp_key_grad: bfloat16 [16, 2048, 512], P('resp', 'ctx')
- resp_value_grad: bfloat16 [16, 2048, 512], P('resp', 'ctx')
- prompt_key_grad: bfloat16 [512, 512], P('ctx')
- prompt_value_grad: bfloat16 [512, 512], P('ctx')
Inputs may be any that keep to these rules, and one draw needn't show every extreme that they name: `lengths`: some response has all 2048 tokens.
All inputs are finite; a program needn't handle non-finite values.
Results may differ from a plain program's by a relative error of at most 0.023.
Values may be sent and summed in bfloat16 or wider, within the bound.
A program may use at most 128 MiB of HBM per device.

v0:
```python
import math
import jax
import jax.numpy as jnp
from jax import lax
from jax.sharding import PartitionSpec as P

DH = 128
HQ = 20
HK = 4
NEG = -1e30


def score_block(query4, keys_blk, key_pos, row_pos, scale):
    keys3 = keys_blk.reshape(keys_blk.shape[0], query4.shape[1], query4.shape[3])
    raw = jnp.einsum("nkgd,mkd->kgnm", query4, keys3, preferred_element_type=jnp.float32) * scale
    allowed = key_pos[None, :] <= row_pos[:, None]
    return jnp.where(allowed[None, None], raw, jnp.float32(NEG))


def scan_blocks(keys_all, values_all, pos_all, step, init):
    total_rows = keys_all.shape[0]
    block = math.gcd(total_rows, 512)
    count = total_rows // block
    blocks = (
        keys_all.reshape(count, block, keys_all.shape[1]),
        values_all.reshape(count, block, values_all.shape[1]),
        pos_all.reshape(count, block),
    )
    return lax.scan(step, init, blocks)


def body(queries, resp_keys, resp_values, prompt_keys, prompt_values, out_grad, lengths):
    rows = queries.shape[1]
    group = HQ // HK
    width = HK * DH
    scale = DH ** (-0.5)
    cycle = lax.axis_size("ctx")
    first_row = lax.axis_index("ctx") * rows
    row_pos = first_row + jnp.arange(rows, dtype=jnp.int32)
    row_ok = row_pos < lengths[0]
    query4 = queries[0].reshape(rows, HK, group, DH)
    grad = jnp.where(row_ok[:, None], out_grad[0], jnp.zeros_like(out_grad[0]))
    grad4 = grad.reshape(rows, HK, group, DH)
    seq_rows = resp_keys.shape[1] * cycle
    prompt_rows = prompt_keys.shape[0] * cycle

    def stats_update(stats, keys_blk, key_pos):
        top, total = stats
        scores = score_block(query4, keys_blk, key_pos, row_pos, scale)
        new_top = jnp.maximum(top, jnp.max(scores, axis=-1))
        total = total * jnp.exp(top - new_top) + jnp.sum(
            jnp.exp(scores - new_top[..., None]), axis=-1
        )
        return (new_top, total)

    top0 = jnp.full((HK, group, rows), NEG, jnp.float32)
    total0 = jnp.zeros((HK, group, rows), jnp.float32)
    pieces = (
        lax.all_gather(prompt_keys, "ctx", axis=0, tiled=True),
        lax.all_gather(prompt_values, "ctx", axis=0, tiled=True),
    )
    top = top0
    total = total0
    key_pos = jnp.full((pieces[0].shape[0],), -1, jnp.int32)
    top, total = stats_update((top, total), pieces[0], key_pos)
    key_buf = pieces[0]
    value_buf = pieces[1]
    top, total, prompt_kbuf, prompt_vbuf = (top, total, key_buf, value_buf)
    pieces = (
        lax.all_gather(resp_keys[0], "ctx", axis=0, tiled=True),
        lax.all_gather(resp_values[0], "ctx", axis=0, tiled=True),
    )
    top, total, key_buf, value_buf = (
        top,
        total,
        jnp.zeros((seq_rows, width), jnp.bfloat16),
        jnp.zeros((seq_rows, width), jnp.bfloat16),
    )
    key_pos = jnp.arange(pieces[0].shape[0], dtype=jnp.int32)
    top, total = stats_update((top, total), pieces[0], key_pos)
    key_buf = pieces[0]
    value_buf = pieces[1]
    top, total, resp_kbuf, resp_vbuf = (top, total, key_buf, value_buf)
    lse = top + jnp.log(total)
    prompt_pos = jnp.full((prompt_rows,), -1, jnp.int32)
    resp_pos = jnp.arange(seq_rows, dtype=jnp.int32)

    def out_step(acc, blk):
        keys_blk, values_blk, key_pos = blk
        scores = score_block(query4, keys_blk, key_pos, row_pos, scale)
        prob = jnp.exp(scores - lse[..., None]).astype(jnp.bfloat16)
        values3 = values_blk.reshape(values_blk.shape[0], HK, DH)
        return (
            acc + jnp.einsum("kgnm,mkd->nkgd", prob, values3, preferred_element_type=jnp.float32),
            None,
        )

    mixed0 = jnp.zeros((rows, HK, group, DH), jnp.float32)
    mixed, unused = scan_blocks(prompt_kbuf, prompt_vbuf, prompt_pos, out_step, mixed0)
    mixed, unused = scan_blocks(resp_kbuf, resp_vbuf, resp_pos, out_step, mixed)
    attn_out = jnp.where(row_ok[:, None], mixed.reshape(rows, HQ * DH), jnp.float32(0.0)).astype(
        jnp.bfloat16
    )
    delta = jnp.einsum(
        "nkgd,nkgd->kgn",
        grad4,
        attn_out.reshape(rows, HK, group, DH),
        preferred_element_type=jnp.float32,
    )

    def grads_block(keys_blk, values_blk, key_pos):
        scores = score_block(query4, keys_blk, key_pos, row_pos, scale)
        prob = jnp.exp(scores - lse[..., None])
        prob_low = prob.astype(jnp.bfloat16)
        keys3 = keys_blk.reshape(keys_blk.shape[0], HK, DH)
        values3 = values_blk.reshape(values_blk.shape[0], HK, DH)
        dprob = jnp.einsum("nkgd,mkd->kgnm", grad4, values3, preferred_element_type=jnp.float32)
        dscore = (prob * (dprob - delta[..., None])).astype(jnp.bfloat16)
        dquery = (
            jnp.einsum("kgnm,mkd->nkgd", dscore, keys3, preferred_element_type=jnp.float32) * scale
        )
        dkey = (
            jnp.einsum("kgnm,nkgd->mkd", dscore, query4, preferred_element_type=jnp.float32) * scale
        )
        dvalue = jnp.einsum("kgnm,nkgd->mkd", prob_low, grad4, preferred_element_type=jnp.float32)
        both = jnp.concatenate(
            [dkey.reshape(keys_blk.shape[0], width), dvalue.reshape(keys_blk.shape[0], width)],
            axis=1,
        )
        return (dquery, both)

    def back_step(acc, blk):
        keys_blk, values_blk, key_pos = blk
        dquery, both = grads_block(keys_blk, values_blk, key_pos)
        return (acc + dquery, both)

    dquery0 = jnp.zeros((rows, HK, group, DH), jnp.float32)
    dquery, prompt_terms = scan_blocks(prompt_kbuf, prompt_vbuf, prompt_pos, back_step, dquery0)
    prompt_term = prompt_terms.reshape(prompt_rows, 2 * width)
    dquery, resp_terms = scan_blocks(resp_kbuf, resp_vbuf, resp_pos, back_step, dquery)
    resp_sum = lax.psum_scatter(
        resp_terms.reshape(seq_rows, 2 * width), "ctx", scatter_dimension=0, tiled=True
    )
    query_grad = dquery.reshape(rows, HQ * DH).astype(jnp.bfloat16)
    prompt_part = lax.psum_scatter(prompt_term, "ctx", scatter_dimension=0, tiled=True)
    prompt_sum = lax.psum(prompt_part, "resp")
    resp_key_grad = resp_sum[:, :width].astype(jnp.bfloat16)
    resp_value_grad = resp_sum[:, width:].astype(jnp.bfloat16)
    prompt_key_grad = prompt_sum[:, :width].astype(jnp.bfloat16)
    prompt_value_grad = prompt_sum[:, width:].astype(jnp.bfloat16)
    return (
        attn_out[None],
        query_grad[None],
        resp_key_grad[None],
        resp_value_grad[None],
        prompt_key_grad,
        prompt_value_grad,
    )


def solution(mesh):
    in_specs = (
        P("resp", "ctx", None),
        P("resp", "ctx", None),
        P("resp", "ctx", None),
        P("ctx", None),
        P("ctx", None),
        P("resp", "ctx", None),
        P("resp"),
    )
    out_specs = (
        P("resp", "ctx", None),
        P("resp", "ctx", None),
        P("resp", "ctx", None),
        P("resp", "ctx", None),
        P("ctx", None),
        P("ctx", None),
    )
    return jax.shard_map(body, mesh=mesh, in_specs=in_specs, out_specs=out_specs, check_vma=False)
```

profile of v0, /device:TPU:8, one launch (start us, length us, event | category | flops | bytes accessed | tf_op | source)
XLA Modules:
  0.0 321.6 jit_solution(5401829585454170042)
XLA Ops:
  11.4 23.7 %all_gather.12 = bf16[512,512]{1,0:T(8,128)(2,1)S(1)} all-gather(bf16[32,512]{1,0:T(8,128)(2,1)} %param.14), channel_id=1, replica_groups=mesh['resp'=16,'ctx'=16] {'ctx'}, dimensions={0}, use_global_device_ids=true | all-gather | bytes 557056 | tf_op jit(solution)/shard_map/all_gather | solution.py:59
  35.3 20.1 %all_gather.14 = bf16[512,512]{1,0:T(8,128)(2,1)S(1)} all-gather(bf16[32,512]{1,0:T(8,128)(2,1)} %param.15), channel_id=1, replica_groups=mesh['resp'=16,'ctx'=16] {'ctx'}, dimensions={0}, use_global_device_ids=true | all-gather | bytes 557056 | tf_op jit(solution)/shard_map/all_gather | solution.py:60
  58.5 3.2 bitcast_reduce_fusion
  61.7 4.8 %fusion.39 = (f32[4,5,128]{2,1,0:T(8,128)S(1)}, f32[4,2048,128,5]{2,1,3,0:T(8,128)S(1)}) fusion(pred[128,2048]{0,1:T(8,128)(4,1)S(1)} %iota_compare_fusion, bf16[2048,4,128,1]{0,2,3,1:T(8,128)(2,1)} %bitcast.261, bf16[128,4,5,128]{0,3,2,1:T(8,128)(2,1)S(1)} %bitcast.245), kind=kOutput, calls=%fused_computation.49 | convolution fusion | flops 1357903360 | bytes 23996416 | tf_op jit(solution)/shard_map/nkgd,mkd->kgnm/dot_general | solution.py:15
  66.5 3.7 %fusion.43 = f32[4,5,128]{2,1,0:T(8,128)S(1)} fusion(f32[4,512,128,5]{2,1,3,0:T(8,128)} %get-tuple-element.374, f32[4,5,128]{2,1,0:T(8,128)S(1)} %get-tuple-element.371, pred[128]{0:T(512)(128)(4,1)S(1)} %broadcast_compare_fusion.2), kind=kLoop, calls=%fused_computation.56 | loop fusion | flops 5240320 | bytes 5263488 | tf_op jit(solution)/shard_map/reduce_sum | solution.py:51
  70.2 4.5 %exponential_reduce_fusion = f32[4,5,128]{2,1,0:T(8,128)S(1)} fusion(f32[4,2048,128,5]{2,1,3,0:T(8,128)S(1)} %get-tuple-element.376, f32[4,5,128]{2,1,0:T(8,128)S(1)} %get-tuple-element.372, pred[128,2048]{0,1:T(8,128)(4,1)S(1)} %iota_compare_fusion), kind=kLoop, calls=%fused_computation.48 | loop fusion | flops 20968960 | bytes 21254144 | tf_op jit(solution)/shard_map/reduce_sum | solution.py:51
  79.6 4.5 %reshape.290 = bf16[4,512,512]{1,0,2:T(4,128)(2,1)} reshape(bf16[1,2048,512]{1,2,0:T(8,128)(2,1)} %all-gather.5.cloned.1.call-done) | data formatting | bytes 4194304 | tf_op jit(solution)/shard_map/reshape | solution.py:25
  84.1 3.3 %copy.171 = bf16[4,512,512]{1,2,0:T(8,128)(2,1)} copy(bf16[4,512,512]{1,0,2:T(4,128)(2,1)} %reshape.290) | data formatting | bytes 4194304
  87.5 6.5 %all-gather.7.cloned.1.call-done = bf16[1,2048,512]{2,1,0:T(8,128)(2,1)} async-done(((bf16[1,128,512]{2,1,0:T(8,128)(2,1)}), bf16[1,2048,512]{2,1,0:T(8,128)(2,1)}) %all-gather.7.cloned.1.call-update) | async-done | bytes 2097168 | tf_op jit(solution)/shard_map/all_gather | solution.py:71
  93.9 4.1 %copy.170 = bf16[4,512,512]{1,2,0:T(8,128)(2,1)} copy(bf16[4,512,512]{2,1,0:T(8,128)(2,1)} %bitcast.267) | data formatting | bytes 4194304
  98.1 21.0 %while.6 = (s32[]{:T(128)}, f32[128,4,5,128]{0,3,2,1:T(8,128)S(1)}, bf16[4,512,512]{1,2,0:T(8,128)(2,1)}, s32[4,512]{1,0:T(4,128)S(1)}, bf16[4,512,512]{1,2,0:T(...) while((s32[]{:T(128)}, ...), condition=%wide.region_5.6_spmd.clone, body=%wide.region_4.5_spmd.clone.sunk | while | flops 676724864 | bytes 6571113 | solution.py:29
  100.1 3.1 fusion.108
  105.3 3.1 fusion.108
  110.6 3.1 fusion.108
  115.8 3.1 fusion.108
  121.1 5.3 %fusion.50 = f32[4,128,512,1]{2,1,3,0:T(8,128)} fusion(bf16[128,4,5,128]{0,3,2,1:T(8,128)(2,1)S(1)} %get-tuple-element.536, f32[4,512,128,5]{2,1,3,0:T(8,128)} %get-tuple-element.374, f32[4,5,128]{2,1,0:T(8,128)} %get-tuple-element.581, pred[128]{0:T(512)(128)(4,1)S(1)} %broadcast_compare_fusion.3), kind=kOutput, calls=%fused_computation.75 | convolution fusion | flops 340787200 | bytes 6957184 | tf_op jit(solution)/shard_map/while/body/eval_jaxpr/kgnm,nkgd->mkd/dot_general | solution.py:125
  133.9 3.1 pad_maximum_fusion
  138.6 69.7 %while.7 = (s32[]{:T(128)}, f32[128,4,5,128]{0,3,2,1:T(8,128)}, f32[4,512,1024]{2,1,0:T(8,128)}, bf16[4,512,512]{1,2,0:T(8,128)(2,1)}, s32[4,512]{1,0:T(4,128)S(...) while((s32[]{:T(128)}, f32[128,4,5,128]{0,3,2,1:T(8,128)}, ...), condition=%wide.region_7.8_spmd.clone, body=%wide.region_6.7_spmd.clone.sunk | while | flops 1692336256 | bytes 52139704 | solution.py:29
  146.7 2.9 copy.245
  149.6 3.2 constant_dynamic-update-slice_fusion.2
  152.8 3.2 fusion.121
  164.1 2.9 copy.245
  167.0 3.2 constant_dynamic-update-slice_fusion.2
  170.2 3.2 fusion.121
  181.5 2.9 copy.245
  184.4 3.2 constant_dynamic-update-slice_fusion.2
  187.6 3.2 fusion.121
  198.9 2.9 copy.245
  201.8 3.2 constant_dynamic-update-slice_fusion.2
  205.0 3.2 fusion.121
  211.9 81.9 %all-reduce.1 = bf16[32,1024]{1,0:T(8,128)(2,1)S(1)} all-reduce(f32[32,1024]{1,0:T(8,128)} %reduce-scatter.5.cloned.1.call-done), channel_id=1, replica_groups=mesh['resp'=16,'ctx'=16] {'resp'}, use_global_device_ids=true, to_apply=%region_10.11 | all-reduce | flops 32768 | bytes 196608 | tf_op jit(solution)/shard_map/psum | solution.py:146
  294.5 18.8 %reduce-scatter.3.cloned.1.call-done = f32[128,1024]{1,0:T(8,128)} async-done(((f32[2048,1024]{1,0:T(8,128)}), f32[128,1024]{1,0:T(8,128)}) %reduce-scatter.3.cloned.1.call-update) | async-done | bytes 524304 | tf_op jit(solution)/shard_map/reduce_scatter | solution.py:141
  (143 shorter events, 69.0 us)
Async XLA Ops:
  7.2 50.2 %copy-start.4 = (bf16[1,128,2560]{2,1,0:T(8,128)(2,1)S(1)}, bf16[1,128,2560]{2,1,0:T(8,128)(2,1)}, u32[]{:S(2)}) copy-start(bf16[1,128,2560]{2,1,0:T(8,128)(2,1)} %param.16) | copy-start | bytes 1966084
  7.2 54.5 %all-gather.5.cloned.1.call-start = ((), (), s32[]{:S(2)}) async-start(), calls=%async_computation.4 | async-start | bytes 2228224 | tf_op jit(solution)/shard_map/all_gather | solution.py:70
  9.0 85.0 %all-gather.7.cloned.1.call-start = ((), (), s32[]{:S(2)}) async-start(), calls=%async_computation.5 | async-start | bytes 2228224 | tf_op jit(solution)/shard_map/all_gather | solution.py:71
  9.7 202.2 %reduce-scatter.5.cloned.1.call-start = ((), (), s32[]{:S(2)}) async-start(), calls=%async_computation.3 | async-start | bytes 2228224 | tf_op jit(solution)/shard_map/reduce_scatter | solution.py:145
  55.6 19.1 %copy-start.7 = (bf16[512,512]{0,1:T(8,128)(2,1)}, bf16[512,512]{0,1:T(8,128)(2,1)S(1)}, u32[]{:S(2)}) copy-start(bf16[512,512]{0,1:T(8,128)(2,1)S(1)} %copy.166) | copy-start | bytes 1572868
  66.5 8.9 %slice-start = ((s8[5242880]{0:T(1024)(128)(4,1)}), s8[4194304]{0:T(1024)(128)(4,1)S(1)}, s32[]{:S(2)}) async-start(s8[5242880]{0:T(1024)(128)(4,1)} %bitcast.252), calls=%async_computation.6 | async-start | bytes 8388608
  70.2 5.2 %slice-start.1 = ((s8[5242880]{0:T(1024)(128)(4,1)}), s8[1048576]{0:T(1024)(128)(4,1)S(1)}, s32[]{:S(2)}) async-start(s8[5242880]{0:T(1024)(128)(4,1)} %bitcast.252), calls=%async_computation.7 | async-start | bytes 2097152
  74.8 0.6 copy-start.11
  119.1 7.2 %copy-start.2 = (f32[128,4,5,128]{0,3,2,1:T(8,128)}, f32[128,4,5,128]{0,3,2,1:T(8,128)S(1)}, u32[]{:S(2)}) copy-start(f32[128,4,5,128]{0,3,2,1:T(8,128)S(1)} %get-tuple-element.157) | copy-start | bytes 3932164
  119.1 7.2 %slice-start.2 = ((s8[5242880]{0:T(1024)(128)(4,1)}), s8[4194304]{0:T(1024)(128)(4,1)S(1)}, s32[]{:S(2)}) async-start(s8[5242880]{0:T(1024)(128)(4,1)} %bitcast.254), calls=%async_computation.8 | async-start | bytes 8388608
  119.1 7.2 %copy-start.8 = (bf16[512,512]{0,1:T(8,128)(2,1)S(1)}, bf16[512,512]{0,1:T(8,128)(2,1)}, u32[]{:S(2)}) copy-start(bf16[512,512]{0,1:T(8,128)(2,1)} %copy-done.7) | copy-start | bytes 1572868
  119.1 7.2 %copy-start.12 = (f32[4,5,128]{2,1,0:T(8,128)S(1)}, f32[4,5,128]{2,1,0:T(8,128)}, u32[]{:S(2)}) copy-start(f32[4,5,128]{2,1,0:T(8,128)} %get-tuple-element.581) | copy-start | bytes 30724
  121.0 7.0 %copy-start.5 = (bf16[128,4,5,128]{0,3,2,1:T(8,128)(2,1)}, bf16[128,4,5,128]{0,3,2,1:T(8,128)(2,1)S(1)}, u32[]{:S(2)}) copy-start(bf16[128,4,5,128]{0,3,2,1:T(8,128)(2,1)S(1)} %get-tuple-element.536) | copy-start | bytes 1966084
  121.0 7.0 %copy-start.9 = (f32[4,5,128]{2,1,0:T(8,128)}, f32[4,5,128]{2,1,0:T(8,128)S(1)}, u32[]{:S(2)}) copy-start(f32[4,5,128]{2,1,0:T(8,128)S(1)} %get-tuple-element.537) | copy-start | bytes 30724
  121.1 5.3 %slice-start.3 = ((s8[5242880]{0:T(1024)(128)(4,1)}), s8[1048576]{0:T(1024)(128)(4,1)S(1)}, s32[]{:S(2)}) async-start(s8[5242880]{0:T(1024)(128)(4,1)} %bitcast.254), calls=%async_computation.9 | async-start | bytes 2097152
  132.6 5.9 %copy-start.10 = (f32[4,5,128]{2,1,0:T(8,128)S(1)}, f32[4,5,128]{2,1,0:T(8,128)}, u32[]{:S(2)}) copy-start(f32[4,5,128]{2,1,0:T(8,128)} %copy-done.9) | copy-start | bytes 30724
  132.6 5.9 %copy-start.13 = (f32[4,5,128]{2,1,0:T(8,128)S(1)}, f32[4,5,128]{2,1,0:T(8,128)}, u32[]{:S(2)}) copy-start(f32[4,5,128]{2,1,0:T(8,128)} %get-tuple-element.581) | copy-start | bytes 30724
  137.0 176.3 %reduce-scatter.3.cloned.1.call-start = ((), (), s32[]{:S(2)}) async-start(), calls=%async_computation.2 | async-start | bytes 8912896 | tf_op jit(solution)/shard_map/reduce_scatter | solution.py:141
  138.6 2.4 copy-start.6
  139.9 1.1 copy-start
  156.0 2.4 copy-start.6
  157.3 1.1 copy-start
  173.4 2.4 copy-start.6
  174.7 1.1 copy-start
  190.8 2.4 copy-start.6
  192.1 1.1 copy-start
  208.2 1.3 copy-start.1
  208.2 2.5 copy-start.3
Sparse Core Ops, SparseCore 0:
  10.4 43.8 all-gather.4
  56.1 37.7 all-gather.6
  137.1 66.8 reduce-scatter.4
  208.4 104.8 reduce-scatter.2
where the time goes:
time: 323 us; the launch traced here: 322 us
  blocking collectives  126 us (39%)
  local copies, waits for them, and re-layouts  65.2 us (20%)
  matrix products  64.7 us (20%)
  waiting for transfers between devices  26 us (8%)
  other arithmetic  24.4 us (8%)
  between operations  14.7 us (5%)
    psum x1, blocking collectives, body(): prompt_sum = lax.psum(prompt_part, 'resp')  81.9 us
    dynamic_update_slice x8, local copies, waits for them, and re-layouts, scan_blocks(): return lax.scan(step, init, blocks)  24.5 us
    all_gather x1, blocking collectives, body(): lax.all_gather(prompt_keys, 'ctx', axis=0, tiled=True)  23.7 us
    all_gather x1, blocking collectives, body(): lax.all_gather(prompt_values, 'ctx', axis=0, tiled=True)  20.1 us
    unnamed x42, local copies, waits for them, and re-layouts  20 us
    reduce_scatter x1, waiting for transfers between devices, body(): lax.psum_scatter(resp_terms.reshape(seq_rows, 2 * width), 'ctx', scatter_...  18.8 us
    dot_general x5, matrix products, out_step(): jnp.einsum('kgnm,mkd->nkgd', prob, values3, preferred_element_type=jnp.fl...  15.1 us
    dot_general x5, matrix products, grads_block(): jnp.einsum('kgnm,mkd->nkgd', dscore, keys3, preferred_element_type=jnp.fl...  13.8 us
  transfers between devices with their start and end apart: 4, of which 2 were waited for; matrix products, arithmetic and copies ran while one was open for 33% of the time, Pallas kernels for 0%

commit v1 on v0

--- a/solution.py
+++ b/solution.py
@@ -143,7 +143,7 @@
     )
     query_grad = dquery.reshape(rows, HQ * DH).astype(jnp.bfloat16)
     prompt_part = lax.psum_scatter(prompt_term, "ctx", scatter_dimension=0, tiled=True)
-    prompt_sum = lax.psum(prompt_part, "resp")
+    prompt_sum = jnp.sum(lax.all_gather(prompt_part, axis_name="resp"), axis=0)
     resp_key_grad = resp_sum[:, :width].astype(jnp.bfloat16)
     resp_value_grad = resp_sum[:, width:].astype(jnp.bfloat16)
     prompt_key_grad = prompt_sum[:, :width].astype(jnp.bfloat16)

time: 323 us -> 382 us (1.18)
  waiting for transfers between devices: 26 us -> 161 us
  blocking collectives: 126 us -> 43.8 us
  matrix products: 64.7 us -> 69.5 us
    psum x1 -> x0, blocking collectives: 81.9 us -> none  [body(): prompt_sum = lax.psum(prompt_part, 'resp')]
    reduce_scatter x1, waiting for transfers between devices: 18.8 us -> 92.6 us  [body(): lax.psum_scatter(resp_terms.reshape(seq_rows, 2 * width), 'ctx', scatter_...]
    reduce_scatter x1, waiting for transfers between devices: 0.01 us -> 60.9 us  [body(): lax.psum_scatter(prompt_term, 'ctx', scatter_dimension=0, tiled=True)]
    unnamed x42 -> x28, local copies, waits for them, and re-layouts: 20 us -> 21.6 us
  transfers between devices with their start and end apart: 4 -> 5, of which waited for: 2 -> 3; matrix products, arithmetic and copies ran while one was open for 33% -> 30% of each run, Pallas kernels for 0% -> 0%
where the time goes in v1:
time: 382 us; the launch traced here: 380 us
  waiting for transfers between devices  161 us (42%)
  matrix products  69.5 us (18%)
  local copies, waits for them, and re-layouts  66.7 us (17%)
  blocking collectives  43.8 us (11%)
  other arithmetic  23.5 us (6%)
  between operations  14.7 us (4%)
    reduce_scatter x1, waiting for transfers between devices, body(): lax.psum_scatter(resp_terms.reshape(seq_rows, 2 * width), 'ctx', scatter_...  92.6 us
    reduce_scatter x1, waiting for transfers between devices, body(): lax.psum_scatter(prompt_term, 'ctx', scatter_dimension=0, tiled=True)  60.9 us
    dynamic_update_slice x8, local copies, waits for them, and re-layouts, scan_blocks(): return lax.scan(step, init, blocks)  24.3 us
    all_gather x1, blocking collectives, body(): lax.all_gather(prompt_keys, 'ctx', axis=0, tiled=True)  23.7 us
    unnamed x28, local copies, waits for them, and re-layouts  21.6 us
    all_gather x1, blocking collectives, body(): lax.all_gather(prompt_values, 'ctx', axis=0, tiled=True)  20.1 us
    dot_general x5, matrix products, grads_block(): jnp.einsum('kgnm,mkd->nkgd', dscore, keys3, preferred_element_type=jnp.fl...  16 us
    dot_general x5, matrix products, out_step(): jnp.einsum('kgnm,mkd->nkgd', prob, values3, preferred_element_type=jnp.fl...  15.1 us
  transfers between devices with their start and end apart: 5, of which 3 were waited for; matrix products, arithmetic and copies ran while one was open for 30% of the time, Pallas kernels for 0%

profile of v1, /device:TPU:8, one launch (start us, length us, event | category | flops | bytes accessed | tf_op | source)
XLA Modules:
  0.0 380.5 jit_solution(5974117597414365941)
XLA Ops:
  11.4 23.7 %all_gather.18 = bf16[512,512]{1,0:T(8,128)(2,1)S(1)} all-gather(bf16[32,512]{1,0:T(8,128)(2,1)} %param.14), channel_id=1, replica_groups=mesh['resp'=16,'ctx'=16] {'ctx'}, dimensions={0}, use_global_device_ids=true | all-gather | bytes 557056 | tf_op jit(solution)/shard_map/all_gather | solution.py:59
  35.3 20.1 %all_gather.20 = bf16[512,512]{1,0:T(8,128)(2,1)S(1)} all-gather(bf16[32,512]{1,0:T(8,128)(2,1)} %param.15), channel_id=1, replica_groups=mesh['resp'=16,'ctx'=16] {'ctx'}, dimensions={0}, use_global_device_ids=true | all-gather | bytes 557056 | tf_op jit(solution)/shard_map/all_gather | solution.py:60
  58.5 3.2 bitcast_reduce_fusion
  61.7 4.8 %fusion.39 = (f32[4,5,128]{2,1,0:T(8,128)S(1)}, f32[4,2048,128,5]{2,1,3,0:T(8,128)S(1)}) fusion(pred[128,2048]{0,1:T(8,128)(4,1)S(1)} %iota_compare_fusion, bf16[2048,4,128,1]{0,2,3,1:T(8,128)(2,1)} %bitcast.260, bf16[128,4,5,128]{0,3,2,1:T(8,128)(2,1)S(1)} %bitcast.246), kind=kOutput, calls=%fused_computation.49 | convolution fusion | flops 1357903360 | bytes 23996416 | tf_op jit(solution)/shard_map/nkgd,mkd->kgnm/dot_general | solution.py:15
  66.5 3.7 fusion.43
  70.2 4.5 %exponential_reduce_fusion = f32[4,5,128]{2,1,0:T(8,128)S(1)} fusion(f32[4,2048,128,5]{2,1,3,0:T(8,128)S(1)} %get-tuple-element.376, f32[4,5,128]{2,1,0:T(8,128)S(1)} %get-tuple-element.372, pred[128,2048]{0,1:T(8,128)(4,1)S(1)} %iota_compare_fusion), kind=kLoop, calls=%fused_computation.48 | loop fusion | flops 20968960 | bytes 21254144 | tf_op jit(solution)/shard_map/reduce_sum | solution.py:51
  79.1 4.5 %reshape.290 = bf16[4,512,512]{1,0,2:T(4,128)(2,1)} reshape(bf16[1,2048,512]{1,2,0:T(8,128)(2,1)} %all-gather.7.cloned.1.call-done) | data formatting | bytes 4194304 | tf_op jit(solution)/shard_map/reshape | solution.py:25
  83.6 3.4 copy.169
  87.0 6.9 %all-gather.9.cloned.1.call-done = bf16[1,2048,512]{2,1,0:T(8,128)(2,1)} async-done(((bf16[1,128,512]{2,1,0:T(8,128)(2,1)}), bf16[1,2048,512]{2,1,0:T(8,128)(2,1)}) %all-gather.9.cloned.1.call-update) | async-done | bytes 2097168 | tf_op jit(solution)/shard_map/all_gather | solution.py:71
  93.9 4.1 %copy.168 = bf16[4,512,512]{1,2,0:T(8,128)(2,1)} copy(bf16[4,512,512]{2,1,0:T(8,128)(2,1)} %bitcast.267) | data formatting | bytes 4194304
  98.0 18.5 %while.6 = (s32[]{:T(128)}, f32[128,4,5,128]{0,3,2,1:T(8,128)S(1)}, bf16[4,512,512]{1,2,0:T(8,128)(2,1)}, s32[4,512]{1,0:T(4,128)S(1)}, bf16[4,512,512]{1,2,0:T(...) while((s32[]{:T(128)}, ...), condition=%wide.region_5.6_spmd.clone, body=%wide.region_4.5_spmd.clone.sunk | while | flops 676724864 | bytes 6571113 | solution.py:29
  99.5 3.1 fusion.108
  104.1 3.1 fusion.108
  108.6 3.1 fusion.108
  113.2 3.1 fusion.108
  119.3 3.8 %fusion.50 = f32[4,128,512,1]{2,1,3,0:T(8,128)S(1)} fusion(bf16[128,4,5,128]{0,3,2,1:T(8,128)(2,1)S(1)} %get-tuple-element.536, f32[4,512,128,5]{2,1,3,0:T(8,128)} %get-tuple-element.374, f32[4,5,128]{2,1,0:T(8,128)S(1)} %get-tuple-element.585, pred[128]{0:T(512)(128)(4,1)S(1)} %broadcast_compare_fusion.3), kind=kOutput, calls=%fused_computation.75 | convolution fusion | flops 340787200 | bytes 6957184 | tf_op jit(solution)/shard_map/while/body/eval_jaxpr/kgnm,nkgd->mkd/dot_general | solution.py:125
  124.5 4.5 %fusion.41 = bf16[4,5,128,512]{2,3,1,0:T(8,128)(2,1)S(1)} fusion(f32[4,512,128,5]{2,1,3,0:T(8,128)} %get-tuple-element.374, f32[4,5,128]{2,1,0:T(8,128)S(1)} %get-tuple-element.537, f32[4,5,128]{2,1,0:T(8,128)S(1)} %get-tuple-element.585, pred[128]{0:T(512)(128)(4,1)S(1)} %broadcast_compare_fusion.3, bf16[128,4,5,128]{0,3,2,1:T(8,128)(2,1)} %copy-done.6, ...), kind=kOutput, calls=%fused_computation.52 | convolution fusion | flops 343408640 | bytes 9064576 | tf_op jit(solution)/shard_map/while/body/eval_jaxpr/nkgd,mkd->kgnm/dot_general | solution.py:117
  133.6 3.1 pad_maximum_fusion
  136.7 3.2 fusion.46
  142.7 60.9 %reduce-scatter.5.cloned.1.call-done = f32[32,1024]{1,0:T(8,128)} async-done(((f32[512,1024]{1,0:T(8,128)}), f32[32,1024]{1,0:T(8,128)}) %reduce-scatter.5.cloned.1.call-update) | async-done | bytes 131088 | tf_op jit(solution)/shard_map/reduce_scatter | solution.py:145
  203.7 69.7 %while.7 = (s32[]{:T(128)}, f32[128,4,5,128]{0,3,2,1:T(8,128)}, f32[4,512,1024]{2,1,0:T(8,128)}, bf16[4,512,512]{1,2,0:T(8,128)(2,1)}, s32[4,512]{1,0:T(4,128)S(...) while((s32[]{:T(128)}, f32[128,4,5,128]{0,3,2,1:T(8,128)}, ...), condition=%wide.region_7.8_spmd.clone, body=%wide.region_6.7_spmd.clone.sunk | while | flops 1692336256 | bytes 52139704 | solution.py:29
  212.1 2.9 copy.244
  214.9 3.2 constant_dynamic-update-slice_fusion.2
  218.2 3.2 fusion.121
  229.4 2.9 copy.244
  232.3 3.2 constant_dynamic-update-slice_fusion.2
  235.5 3.2 fusion.121
  249.6 3.2 constant_dynamic-update-slice_fusion.2
  252.9 3.2 fusion.121
  267.1 3.2 constant_dynamic-update-slice_fusion.2
  270.3 3.2 fusion.121
  279.5 92.6 %reduce-scatter.3.cloned.1.call-done = f32[128,1024]{1,0:T(8,128)} async-done(((f32[2048,1024]{1,0:T(8,128)}), f32[128,1024]{1,0:T(8,128)}) %reduce-scatter.3.cloned.1.call-update) | async-done | bytes 524304 | tf_op jit(solution)/shard_map/reduce_scatter | solution.py:141
  (131 shorter events, 74.0 us)
Async XLA Ops:
  7.2 50.2 %copy-start.5 = (bf16[1,128,2560]{2,1,0:T(8,128)(2,1)S(1)}, bf16[1,128,2560]{2,1,0:T(8,128)(2,1)}, u32[]{:S(2)}) copy-start(bf16[1,128,2560]{2,1,0:T(8,128)(2,1)} %param.16) | copy-start | bytes 1966084
  7.2 54.5 %all-gather.7.cloned.1.call-start = ((), (), s32[]{:S(2)}) async-start(), calls=%async_computation.4 | async-start | bytes 2228224 | tf_op jit(solution)/shard_map/all_gather | solution.py:70
  9.0 84.9 %all-gather.9.cloned.1.call-start = ((), (), s32[]{:S(2)}) async-start(), calls=%async_computation.5 | async-start | bytes 2228224 | tf_op jit(solution)/shard_map/all_gather | solution.py:71
  9.7 193.9 %reduce-scatter.5.cloned.1.call-start = ((), (), s32[]{:S(2)}) async-start(), calls=%async_computation.3 | async-start | bytes 2228224 | tf_op jit(solution)/shard_map/reduce_scatter | solution.py:145
  35.3 26.4 %copy-start.4 = (bf16[512,512]{0,1:T(8,128)(2,1)}, bf16[512,512]{0,1:T(8,128)(2,1)S(1)}, u32[]{:S(2)}) copy-start(bf16[512,512]{0,1:T(8,128)(2,1)S(1)} %copy.157) | copy-start | bytes 1572868
  55.6 19.1 %copy-start.8 = (bf16[512,512]{0,1:T(8,128)(2,1)}, bf16[512,512]{0,1:T(8,128)(2,1)S(1)}, u32[]{:S(2)}) copy-start(bf16[512,512]{0,1:T(8,128)(2,1)S(1)} %copy.164) | copy-start | bytes 1572868
  66.5 8.3 %slice-start = ((s8[5242880]{0:T(1024)(128)(4,1)}), s8[4194304]{0:T(1024)(128)(4,1)S(1)}, s32[]{:S(2)}) async-start(s8[5242880]{0:T(1024)(128)(4,1)} %bitcast.253), calls=%async_computation.7 | async-start | bytes 8388608
  70.2 4.6 %slice-start.1 = ((s8[5242880]{0:T(1024)(128)(4,1)}), s8[1048576]{0:T(1024)(128)(4,1)S(1)}, s32[]{:S(2)}) async-start(s8[5242880]{0:T(1024)(128)(4,1)} %bitcast.253), calls=%async_computation.8 | async-start | bytes 2097152
  116.6 6.5 %copy-start.2 = (f32[128,4,5,128]{0,3,2,1:T(8,128)}, f32[128,4,5,128]{0,3,2,1:T(8,128)S(1)}, u32[]{:S(2)}) copy-start(f32[128,4,5,128]{0,3,2,1:T(8,128)S(1)} %get-tuple-element.157) | copy-start | bytes 3932164
  118.4 0.8 copy-start.6
  136.7 140.5 %all-gather.11.cloned.1.call-start = ((), (), s32[]{:S(2)}) async-start(), calls=%async_computation.6 | async-start | bytes 2228224 | tf_op jit(solution)/shard_map/all_gather | solution.py:146
  203.7 168.5 %reduce-scatter.3.cloned.1.call-start = ((), (), s32[]{:S(2)}) async-start(), calls=%async_computation.2 | async-start | bytes 8912896 | tf_op jit(solution)/shard_map/reduce_scatter | solution.py:141
  203.9 2.4 copy-start.7
  205.3 1.1 copy-start
  221.3 2.4 copy-start.7
  222.7 1.1 copy-start
  238.7 2.4 copy-start.7
  240.0 1.1 copy-start
  256.1 2.4 copy-start.7
  257.4 1.1 copy-start
  273.4 1.3 copy-start.1
  273.5 2.5 copy-start.3
Sparse Core Ops, SparseCore 0:
  10.4 43.9 all-gather.6
  56.2 37.6 all-gather.8
  136.8 66.8 reduce-scatter.4
  205.9 57.2 all-gather.10
  273.6 98.4 reduce-scatter.2
